TPU v7x, 32 devices: a whole 2x2x4 slice. The times are simulated.
32 devices in a mesh: group: 2 (over y), pool: 4 (over x, core), tensor: 4 (over z).
Axes of the slice: x: 2, y: 2, z: 4, core: 2. Of those that a mesh axis runs over, the one named last changes fastest.
Arguments:
- tokens: bfloat16 [8192, 8192], P(('group', 'pool'), 'tensor'), parts along dimension 0, may hold values from -6 to 6
- base_projection_weight: bfloat16 [8192, 2048], P('tensor'), may hold values from -0.09375 to 0.09375
- adapter_down_weight: bfloat16 [64, 8192, 128], P(('group', 'pool'), 'tensor'), parts along dimension 0, may hold values from -0.0625 to 0.0625
- adapter_up_weight: bfloat16 [64, 64, 2048], P(('group', 'pool'), None, 'tensor'), parts along dimension 0, may hold values from -0.75 to 0.75
- batch_adapter_ids: int32 [8, 8], P(('group', 'pool')), parts along dimension 0, may hold values from 0 to 31, as said below
- batch_request_counts: int32 [8, 8], P(('group', 'pool')), parts along dimension 0, may hold values from 1 to 32, 128 in all within a row
- adapter_storage_row: int32 [64], P('group'), parts along dimension 0, may hold values from 0 to 31, as said below
Outputs:
- key_value: bfloat16 [8192, 2048], P(('group', 'pool'), 'tensor'), parts along dimension 0
There are 2 independent parts, one for each index of `group`. A program takes and returns all parts, laid end to end along the dimension named above; an argument that names none is the same for every part. Nothing has to cross between parts.
Inputs may be any that keep to these rules, and one draw needn't show every extreme that they name: `batch_adapter_ids`: within one row (one pool index's batches) the ids are distinct, and exactly 2 of them have adapter_storage_row // 8 equal to each value. A permutation: adapter a lies at row adapter_storage_row[a] of adapter_down_weight and adapter_up_weight, on pool index adapter_storage_row[a] // 8. `batch_request_counts`: each row sums to 128; its largest entry is exactly 32.
All inputs are finite; a program needn't handle non-finite values.
Results may differ from a plain program's by a relative error of at most 0.013.
Values may be sent and summed in bfloat16 or wider, within the bound.
A program may use at most 128 MiB of HBM per device.

v0:
```python
import jax
import jax.numpy as jnp
from jax import lax
from jax.sharding import PartitionSpec as P

KEY_VALUE_WIDTH = 1024
ADAPTER_RANK = 64
DRAFT = 8
CAP = 2


def place_rows(running_totals, values, starting_row, length):
    within_batch = (jnp.arange(values.shape[0]) < length)[:, None]
    prior_count = lax.dynamic_slice_in_dim(running_totals, starting_row, values.shape[0], 0)
    return lax.dynamic_update_slice_in_dim(
        running_totals, prior_count + jnp.where(within_batch, values, 0.0), starting_row, 0
    )


def body(
    tokens,
    base_projection_weight,
    adapter_down_weight,
    adapter_up_weight,
    batch_adapter_ids,
    batch_request_counts,
    adapter_storage_row,
):
    tok_rows = tokens.shape[0]
    feature_part = tokens.shape[1]
    output_columns = adapter_up_weight.shape[2]
    local_slot_count = adapter_down_weight.shape[0]
    batches = batch_adapter_ids.shape[1]
    pool_count = lax.axis_size("pool")
    max_rows = DRAFT * (2 * (tok_rows // DRAFT) // batches)
    counts = batch_request_counts[0]
    starts = (jnp.cumsum(counts) - counts) * DRAFT
    lengths = counts * DRAFT
    storage_index = adapter_storage_row[batch_adapter_ids[0]]
    owners = storage_index // local_slot_count
    local_slot = storage_index % local_slot_count
    batch_index = jnp.arange(batches)
    earlier = (owners[:, None] == owners[None, :]) & (batch_index[None, :] < batch_index[:, None])
    position = jnp.sum(earlier.astype(jnp.int32), axis=1)
    flat_slot = owners * CAP + position
    slot_match = flat_slot[None, :] == jnp.arange(pool_count * CAP)[:, None]
    request = jnp.sum(jnp.where(slot_match, local_slot[None, :], 0), axis=1)
    requested_adapter = lax.all_to_all(
        request.reshape(pool_count, CAP), "pool", split_axis=0, concat_axis=0, tiled=True
    )
    padded = jnp.concatenate([tokens, jnp.zeros((max_rows, feature_part), tokens.dtype)], 0)
    partial_sum = jnp.dot(tokens, base_projection_weight, preferred_element_type=jnp.float32)
    base_accumulator = lax.psum_scatter(
        partial_sum.astype(jnp.bfloat16), "tensor", scatter_dimension=1, tiled=True
    ).astype(jnp.float32)
    down_got, up_got = (
        lax.all_to_all(
            adapter_down_weight[requested_adapter], "pool", split_axis=0, concat_axis=0, tiled=True
        ),
        lax.all_to_all(
            adapter_up_weight[requested_adapter], "pool", split_axis=0, concat_axis=0, tiled=True
        ),
    )
    down_got = down_got.reshape((pool_count * CAP,) + down_got.shape[2:])

    def segment_shrink(batch_position):
        segment = lax.dynamic_slice_in_dim(padded, starts[batch_position], max_rows, 0)
        adapter_block = lax.dynamic_index_in_dim(
            down_got, flat_slot[batch_position], 0, keepdims=False
        )
        return jnp.dot(segment, adapter_block, preferred_element_type=jnp.float32)

    up_got = up_got.reshape((pool_count * CAP,) + up_got.shape[2:])

    def shrink_step(batch_position, running_totals):
        return place_rows(
            running_totals,
            segment_shrink(batch_position),
            starts[batch_position],
            lengths[batch_position],
        )

    shrink_totals = lax.fori_loop(
        0, batches, shrink_step, jnp.zeros((tok_rows + max_rows, 2 * ADAPTER_RANK), jnp.float32)
    )
    shared = lax.psum(shrink_totals[:tok_rows].astype(jnp.bfloat16), "tensor")
    shared_padded = jnp.concatenate(
        [shared, jnp.zeros((max_rows, 2 * ADAPTER_RANK), jnp.bfloat16)], 0
    )
    key_columns = lax.axis_index("tensor") * output_columns < KEY_VALUE_WIDTH

    def expand_step(batch_position, running_totals):
        segment = lax.dynamic_slice_in_dim(shared_padded, starts[batch_position], max_rows, 0)
        half_rank = jnp.where(key_columns, segment[:, :ADAPTER_RANK], segment[:, ADAPTER_RANK:])
        adapter_block = lax.dynamic_index_in_dim(
            up_got, flat_slot[batch_position], 0, keepdims=False
        )
        product = jnp.dot(half_rank, adapter_block, preferred_element_type=jnp.float32)
        return place_rows(running_totals, product, starts[batch_position], lengths[batch_position])

    adapter_accumulator = lax.fori_loop(
        0, batches, expand_step, jnp.zeros((tok_rows + max_rows, output_columns), jnp.float32)
    )[:tok_rows]
    return (base_accumulator + adapter_accumulator).astype(jnp.bfloat16)


def solution(mesh):
    in_specs = (
        P(("group", "pool"), "tensor"),
        P("tensor", None),
        P(("group", "pool"), "tensor", None),
        P(("group", "pool"), None, "tensor"),
        P(("group", "pool"), None),
        P(("group", "pool"), None),
        P("group"),
    )
    out_specs = P(("group", "pool"), "tensor")
    return jax.shard_map(body, mesh=mesh, in_specs=in_specs, out_specs=out_specs, check_vma=False)
```

profile of v0, /device:TPU:0, one launch (start us, length us, event | category | flops | bytes accessed | tf_op | source)
XLA Modules:
  0.0 283.6 jit_solution(4110024930064423777)
XLA Ops:
  6.5 0.7 fusion.12
  7.3 1.3 gather_fusion
  9.0 7.8 %all_to_all.22 = s32[4,1,2]{2,1,0:T(1,128)S(1)} all-to-all(s32[4,1,2]{2,1,0:T(1,128)S(1)} %bitcast.53), channel_id=1, replica_groups=mesh['group'=2,'pool'=4,'tensor'=4] {'pool'}, dimensions={0} | all-to-all | bytes 64 | tf_op jit(solution)/shard_map/all_to_all | solution.py:48
  17.0 5.3 %gather_fusion.1 = bf16[8,2048,128]{2,1,0:T(8,128)(2,1)} fusion(bf16[8,2048,128]{2,1,0:T(8,128)(2,1)} %param.13, s32[1024]{0:T(1024)S(1)} %pad_clamp_fusion), kind=kCustom, calls=%fused_computation.1 | custom fusion | bytes 8388640 | tf_op jit(solution)/shard_map/gather | solution.py:58
  22.4 5.0 %all-to-all-start.1 = ((bf16[4,2,2048,128]{3,2,1,0:T(8,128)(2,1)}), bf16[4,2,2048,128]{3,2,1,0:T(8,128)(2,1)}, u32[]{:S(2)}, u32[]{:S(2)}) async-start(bf16[4,2,2048,128]{3,2,1,0:T(8,128)(2,1)} %bitcast.51), calls=%async_computation.2 | async-start | bytes 8388608 | tf_op jit(solution)/shard_map/all_to_all | solution.py:57
  27.6 5.2 %concatenate.6 = bf16[1280,2048]{1,0:T(8,128)(2,1)} pad(bf16[1024,2048]{1,0:T(8,128)(2,1)} %param.11, bf16[]{:T(256)} %constant.122.clone.1), padding=0_256x0_0 | pad | bytes 9437186 | tf_op jit(solution)/shard_map/concatenate | solution.py:51
  32.8 42.8 %all-to-all-done.1 = bf16[4,2,2048,128]{3,2,1,0:T(8,128)(2,1)} async-done(((bf16[4,2,2048,128]{3,2,1,0:T(8,128)(2,1)}), bf16[4,2,2048,128]{3,2,1,0:T(8,128)(2,1)}, u32[]{:S(2)}, u32[]{:S(2)}) %all-to-all-start.1) | async-done | bytes 4194336 | tf_op jit(solution)/shard_map/all_to_all | solution.py:57
  75.6 73.9 %while.26 = (s32[]{:T(128)}, f32[1280,128]{1,0:T(8,128)S(1)}, s32[8]{0:T(128)S(1)}, s32[8]{0:T(128)S(1)}, bf16[1280,2048]{1,0:T(8,128)(2,1)}, /*index=5*/s32[8]{...) while((s32[]{:T(128)}, f32[1280,128]{1,0:T(8,128)S(1)}, ...), condition=%wide.region_5.6_spmd, body=%wide.region_4.5_spmd.sunk | while | flops 134283520 | bytes 2099421 | solution.py:83
  78.2 0.7 dynamic_slice.115
  80.8 0.7 dynamic_slice.116
  82.1 1.8 fusion.23
  83.9 1.0 dynamic_update_slice.16
  87.5 0.7 dynamic_slice.115
  90.1 0.7 dynamic_slice.116
  91.4 1.8 fusion.23
  93.2 1.0 dynamic_update_slice.16
  96.8 0.7 dynamic_slice.115
  99.3 0.7 dynamic_slice.116
  100.6 1.8 fusion.23
  102.5 1.0 dynamic_update_slice.16
  106.1 0.7 dynamic_slice.115
  108.6 0.7 dynamic_slice.116
  109.9 1.8 fusion.23
  111.7 1.0 dynamic_update_slice.16
  115.3 0.7 dynamic_slice.115
  117.9 0.7 dynamic_slice.116
  119.2 1.8 fusion.23
  121.0 1.0 dynamic_update_slice.16
  124.6 0.7 dynamic_slice.115
  127.2 0.7 dynamic_slice.116
  128.5 1.8 fusion.23
  130.3 1.0 dynamic_update_slice.16
  133.9 0.7 dynamic_slice.115
  136.5 0.7 dynamic_slice.116
  137.8 1.8 fusion.23
  139.6 1.0 dynamic_update_slice.16
  143.2 0.7 dynamic_slice.115
  145.7 0.7 dynamic_slice.116
  147.0 1.8 fusion.23
  149.5 0.7 slice.32
  150.3 13.8 %convolution_convert_fusion = bf16[1024,2048]{1,0:T(8,128)(2,1)} fusion(bf16[1024,2048]{1,0:T(8,128)(2,1)} %param.11, bf16[2048,2048]{1,0:T(8,128)(2,1)} %param.12), kind=kOutput, calls=%fused_computation.19 | convolution fusion | flops 8592031744 | bytes 16777216 | tf_op jit(solution)/shard_map/dot_general | solution.py:52
  164.2 1.4 gather_fusion.2
  165.6 3.5 %all-to-all-start.2 = ((bf16[4,2,64,512]{3,2,1,0:T(8,128)(2,1)}), bf16[4,2,64,512]{3,2,1,0:T(8,128)(2,1)S(1)}, u32[]{:S(2)}, u32[]{:S(2)}) async-start(bf16[4,2,64,512]{3,2,1,0:T(8,128)(2,1)} %bitcast.17), calls=%async_computation.3 | async-start | bytes 1048576 | tf_op jit(solution)/shard_map/all_to_all | solution.py:60
  169.0 17.0 %all-reduce.4.cloned.1.call-done = bf16[1024,128]{1,0:T(8,128)(2,1)} async-done(((bf16[1024,128]{1,0:T(8,128)(2,1)}), bf16[1024,128]{1,0:T(8,128)(2,1)}) %all-reduce.4.cloned.1.call-update) | async-done | bytes 262160 | tf_op jit(solution)/shard_map/psum | solution.py:86
  186.0 1.0 concatenate.7
  187.0 1.9 broadcast_in_dim.88
  188.9 84.7 %while.27 = (s32[]{:T(128)}, f32[1280,512]{1,0:T(8,128)}, s32[8]{0:T(128)S(1)}, s32[8]{0:T(128)S(1)}, pred[]{:T(512)}, /*index=5*/bf16[1280,128]{1,0:T(8,128)(2,...) while((s32[]{:T(128)}, f32[1280,512]{1,0:T(8,128)}, ...), condition=%wide.region_8.9_spmd, body=%wide.region_7.8_spmd.sunk | while | flops 17056008 | bytes 2296826 | solution.py:101
  195.2 1.3 fusion.25
  196.6 3.0 %dynamic_update_slice.17 = f32[1280,512]{1,0:T(8,128)} dynamic-update-slice(f32[1280,512]{1,0:T(8,128)} %get-tuple-element.443, f32[256,512]{1,0:T(8,128)S(1)} %fusion.25, s32[]{:T(128)S(6)} %select_n.172, s32[]{:T(128)} %constant.119.clone.1..sunk.1) | dynamic-update-slice | bytes 1048580 | tf_op jit(solution)/shard_map/while/body/eval_jaxpr/dynamic_update_slice | solution.py:15
  205.9 1.3 fusion.25
  207.2 3.0 %dynamic_update_slice.17 = f32[1280,512]{1,0:T(8,128)} dynamic-update-slice(f32[1280,512]{1,0:T(8,128)} %get-tuple-element.443, f32[256,512]{1,0:T(8,128)S(1)} %fusion.25, s32[]{:T(128)S(6)} %select_n.172, s32[]{:T(128)} %constant.119.clone.1..sunk.1) | dynamic-update-slice | bytes 1048580 | tf_op jit(solution)/shard_map/while/body/eval_jaxpr/dynamic_update_slice | solution.py:15
  216.5 1.3 fusion.25
  217.9 3.0 %dynamic_update_slice.17 = f32[1280,512]{1,0:T(8,128)} dynamic-update-slice(f32[1280,512]{1,0:T(8,128)} %get-tuple-element.443, f32[256,512]{1,0:T(8,128)S(1)} %fusion.25, s32[]{:T(128)S(6)} %select_n.172, s32[]{:T(128)} %constant.119.clone.1..sunk.1) | dynamic-update-slice | bytes 1048580 | tf_op jit(solution)/shard_map/while/body/eval_jaxpr/dynamic_update_slice | solution.py:15
  227.1 1.3 fusion.25
  228.5 3.0 %dynamic_update_slice.17 = f32[1280,512]{1,0:T(8,128)} dynamic-update-slice(f32[1280,512]{1,0:T(8,128)} %get-tuple-element.443, f32[256,512]{1,0:T(8,128)S(1)} %fusion.25, s32[]{:T(128)S(6)} %select_n.172, s32[]{:T(128)} %constant.119.clone.1..sunk.1) | dynamic-update-slice | bytes 1048580 | tf_op jit(solution)/shard_map/while/body/eval_jaxpr/dynamic_update_slice | solution.py:15
  237.8 1.3 fusion.25
  239.2 3.0 %dynamic_update_slice.17 = f32[1280,512]{1,0:T(8,128)} dynamic-update-slice(f32[1280,512]{1,0:T(8,128)} %get-tuple-element.443, f32[256,512]{1,0:T(8,128)S(1)} %fusion.25, s32[]{:T(128)S(6)} %select_n.172, s32[]{:T(128)} %constant.119.clone.1..sunk.1) | dynamic-update-slice | bytes 1048580 | tf_op jit(solution)/shard_map/while/body/eval_jaxpr/dynamic_update_slice | solution.py:15
  248.5 1.3 fusion.25
  249.8 3.0 %dynamic_update_slice.17 = f32[1280,512]{1,0:T(8,128)} dynamic-update-slice(f32[1280,512]{1,0:T(8,128)} %get-tuple-element.443, f32[256,512]{1,0:T(8,128)S(1)} %fusion.25, s32[]{:T(128)S(6)} %select_n.172, s32[]{:T(128)} %constant.119.clone.1..sunk.1) | dynamic-update-slice | bytes 1048580 | tf_op jit(solution)/shard_map/while/body/eval_jaxpr/dynamic_update_slice | solution.py:15
  259.1 1.4 fusion.25
  260.5 3.0 %dynamic_update_slice.17 = f32[1280,512]{1,0:T(8,128)} dynamic-update-slice(f32[1280,512]{1,0:T(8,128)} %get-tuple-element.443, f32[256,512]{1,0:T(8,128)S(1)} %fusion.25, s32[]{:T(128)S(6)} %select_n.172, s32[]{:T(128)} %constant.119.clone.1..sunk.1) | dynamic-update-slice | bytes 1048580 | tf_op jit(solution)/shard_map/while/body/eval_jaxpr/dynamic_update_slice | solution.py:15
  269.8 1.3 fusion.25
  271.1 2.5 dynamic_update_slice.17
  273.6 3.2 %add_convert_fusion = bf16[1024,512]{1,0:T(8,128)(2,1)} fusion(f32[1280,512]{1,0:T(8,128)} %get-tuple-element.269, bf16[1024,512]{1,0:T(8,128)(2,1)} %reduce-scatter.2.cloned.1.call-done), kind=kLoop, calls=%fused_computation.20 | loop fusion | flops 1572864 | bytes 4194304 | tf_op jit(solution)/shard_map/convert_element_type | solution.py:104
  (73 shorter events, 31.3 us)
Async XLA Ops:
  6.5 157.6 %copy-start = (bf16[8,64,512]{2,1,0:T(8,128)(2,1)S(1)}, bf16[8,64,512]{2,1,0:T(8,128)(2,1)}, u32[]{:S(2)}) copy-start(bf16[8,64,512]{2,1,0:T(8,128)(2,1)} %param.14) | copy-start | bytes 1572868
  22.4 5.1 %copy-start.1 = (s32[1,8]{1,0:T(1,128)S(1)}, s32[1,8]{1,0:T(1,128)}, u32[]{:S(2)}) copy-start(s32[1,8]{1,0:T(1,128)} %param.16) | copy-start | bytes 100
  22.4 53.2 %all-to-all-start.1 = ((bf16[4,2,2048,128]{3,2,1,0:T(8,128)(2,1)}), bf16[4,2,2048,128]{3,2,1,0:T(8,128)(2,1)}, u32[]{:S(2)}, u32[]{:S(2)}) async-start(bf16[4,2,2048,128]{3,2,1,0:T(8,128)(2,1)} %bitcast.51), calls=%async_computation.2 | async-start | bytes 8388608 | tf_op jit(solution)/shard_map/all_to_all | solution.py:57
  27.4 158.7 %all-reduce.4.cloned.1.call-start = ((), (), s32[]{:S(2)}) async-start(), calls=%async_computation.5 | async-start | bytes 524288 | tf_op jit(solution)/shard_map/psum | solution.py:86
  150.3 123.3 %reduce-scatter.2.cloned.1.call-start = ((), (), s32[]{:S(2)}) async-start(), calls=%async_computation.4 | async-start | bytes 5242880 | tf_op jit(solution)/shard_map/reduce_scatter | solution.py:53
  165.6 21.5 %all-to-all-start.2 = ((bf16[4,2,64,512]{3,2,1,0:T(8,128)(2,1)}), bf16[4,2,64,512]{3,2,1,0:T(8,128)(2,1)S(1)}, u32[]{:S(2)}, u32[]{:S(2)}) async-start(bf16[4,2,64,512]{3,2,1,0:T(8,128)(2,1)} %bitcast.17), calls=%async_computation.3 | async-start | bytes 1048576 | tf_op jit(solution)/shard_map/all_to_all | solution.py:60
Sparse Core Ops, SparseCore 0:
  150.4 35.6 all-reduce.3
  188.4 76.4 reduce-scatter.1
where the time goes:
time: 286 us; the launch traced here: 284 us
  local copies, waits for them, and re-layouts  78.2 us (27%)
  loops' own time  62.1 us (22%)
  waiting for transfers between devices  59.8 us (21%)
  matrix products  39.1 us (14%)
  other arithmetic  14.7 us (5%)
  between operations  13.5 us (5%)
  starting transfers between devices  8.56 us (3%)
  blocking collectives  7.76 us (3%)
    all_to_all x1, waiting for transfers between devices, body(): lax.all_to_all(adapter_down_weight[requested_adapter], 'pool', split_axis...  42.8 us
    another operation x1, loops' own time, body(): lax.fori_loop(0, batches, expand_step, jnp.zeros((tok_rows + max_rows, ou...  31.3 us
    dynamic_update_slice x16, local copies, waits for them, and re-layouts, place_rows(): lax.dynamic_update_slice_in_dim(running_totals, prior_count + jnp.where(w...  31.2 us
    another operation x1, loops' own time, body(): lax.fori_loop(0, batches, shrink_step, jnp.zeros((tok_rows + max_rows, 2...  30.8 us
    psum x1, waiting for transfers between devices, body(): shared = lax.psum(shrink_totals[:tok_rows].astype(jnp.bfloat16), 'tensor')  17 us
    dot_general x8, matrix products, segment_shrink(): return jnp.dot(segment, adapter_block, preferred_element_type=jnp.float32)  14.5 us
    dot_general x1, matrix products, body(): jnp.dot(tokens, base_projection_weight, preferred_element_type=jnp.float32)  13.8 us
    dot_general x8, matrix products, expand_step(): jnp.dot(half_rank, adapter_block, preferred_element_type=jnp.float32)  10.7 us
  transfers between devices with their start and end apart: 4, of which 2 were waited for; matrix products, arithmetic and copies ran while one was open for 27% of the time, Pallas kernels for 0%

commit v1 on v0

v1 whole, which is shorter than its diff:
```python
import functools

import jax
import jax.numpy as jnp
from jax import lax
from jax.experimental import pallas as pl
from jax.experimental.pallas import tpu as pltpu
from jax.sharding import PartitionSpec as P

DRAFT = 8
CAP = 2
SUBS = 4
HELD = 2
MESH = pl.DeviceIdType.MESH
F32 = jnp.float32
BF16 = jnp.bfloat16


def kernel(
    nz,
    npool,
    tok_hbm,
    w_hbm,
    down_hbm,
    up_hbm,
    ids,
    counts,
    row_table,
    out_hbm,
    tok,
    w,
    down,
    up,
    part,
    right_in,
    left_in,
    down_send,
    down_got,
    up_send,
    up_got,
    shrink,
    shr_right,
    shr_left,
    shr_right_in,
    shr_left_in,
    mixed,
    out_v,
    req_out,
    req_in,
    req_s,
    own_s,
    span_s,
    batch_s,
    tok_sem,
    w_sem,
    down_sem,
    up_sem,
    out_sem,
    part_send,
    right_recv,
    left_recv,
    req_send,
    req_recv,
    req_local,
    down_send_sem,
    down_recv,
    up_send_sem,
    up_recv,
    shr_send_sem,
    shr_right_recv,
    shr_left_recv,
):
    z = lax.axis_index("tensor")
    me = lax.axis_index("pool")
    slots = down_hbm.shape[0]
    batches = ids.shape[1]
    sub = tok.shape[1]
    cw = out_v.shape[2]
    rank2 = down_hbm.shape[2]
    rank = rank2 // 2
    first, last = z == 0, z == nz - 1
    middle = jnp.logical_and(z > 0, z < nz - 1)
    upper = lax.div(2 * z, nz)

    def chunk(i):
        return i + (1 - upper) * (nz - 1 - 2 * i)

    def peer(j):
        return lax.rem(lax.div(me, 2) + lax.div(j, 2), npool // 2) * 2 + lax.rem(me + j, 2)

    def tok_copy(s):
        return pltpu.make_async_copy(tok_hbm.at[pl.ds(s * sub, sub)], tok.at[s], tok_sem.at[s])

    def w_copy(d):
        return pltpu.make_async_copy(
            w_hbm.at[:, pl.ds(pl.multiple_of(d * cw, cw), cw)], w.at[d], w_sem.at[d]
        )

    down_copy = pltpu.make_async_copy(down_hbm, down, down_sem)
    up_copy = pltpu.make_async_copy(up_hbm, up, up_sem)

    def right_copy(d, s):
        return pltpu.make_async_remote_copy(
            src_ref=part.at[d, s],
            dst_ref=right_in.at[d, s],
            send_sem=part_send.at[d, s],
            recv_sem=right_recv.at[d, s],
            device_id={"tensor": z + 1},
            device_id_type=MESH,
        )

    def left_copy(d, s):
        return pltpu.make_async_remote_copy(
            src_ref=part.at[d, s],
            dst_ref=left_in.at[d, s],
            send_sem=part_send.at[d, s],
            recv_sem=left_recv.at[d, s],
            device_id={"tensor": z - 1},
            device_id_type=MESH,
        )

    def shr_right_copy(s):
        return pltpu.make_async_remote_copy(
            src_ref=shr_right.at[s],
            dst_ref=shr_right_in.at[s],
            send_sem=shr_send_sem.at[0, s],
            recv_sem=shr_right_recv.at[s],
            device_id={"tensor": z + 1},
            device_id_type=MESH,
        )

    def shr_left_copy(s):
        return pltpu.make_async_remote_copy(
            src_ref=shr_left.at[s],
            dst_ref=shr_left_in.at[s],
            send_sem=shr_send_sem.at[1, s],
            recv_sem=shr_left_recv.at[s],
            device_id={"tensor": z - 1},
            device_id_type=MESH,
        )

    def pool_copy(src, dst, send, recv, p, landing):
        return pltpu.make_async_remote_copy(
            src_ref=src,
            dst_ref=dst,
            send_sem=send.at[p],
            recv_sem=recv.at[landing],
            device_id={"pool": p},
            device_id_type=MESH,
        )

    def req_copy(p, landing):
        return pool_copy(req_out.at[p], req_in.at[landing], req_send, req_recv, p, landing)

    def down_peer(p, landing):
        return pool_copy(
            down_send.at[p], down_got.at[landing], down_send_sem, down_recv, p, landing
        )

    def up_rows(p):
        return pl.ds(pl.multiple_of(p * rank2, rank2), rank2)

    def up_peer(p, landing):
        return pool_copy(
            up_send.at[p], up_got.at[up_rows(landing)], up_send_sem, up_recv, p, landing
        )

    w_copy(chunk(0)).start()
    for s in range(SUBS):
        tok_copy(s).start()
    down_copy.start()
    up_copy.start()
    for i in range(1, nz):
        w_copy(chunk(i)).start()

    barrier = pltpu.get_barrier_semaphore()

    @pl.when(z > 0)
    def _():
        pl.semaphore_signal(barrier, inc=1, device_id={"tensor": z - 1}, device_id_type=MESH)

    @pl.when(z < nz - 1)
    def _():
        pl.semaphore_signal(barrier, inc=1, device_id={"tensor": z + 1}, device_id_type=MESH)

    for j in range(1, npool):
        p = peer(jnp.int32(j))
        pl.semaphore_signal(barrier, inc=1, device_id={"pool": p}, device_id_type=MESH)

    def read_batch(b, row):
        index = row_table[ids[0, b]]
        batch_s[0, b] = index // slots
        batch_s[1, b] = lax.rem(index, slots)
        batch_s[2, b] = row
        after = row + counts[0, b] * DRAFT
        batch_s[3, b] = after
        return after

    lax.fori_loop(0, batches, read_batch, jnp.int32(0))
    lane8 = lax.broadcasted_iota(jnp.int32, (8, 128), 1)

    def read_holder(p, _):
        def match(b, carry):
            seen, r0, b0, e0, r1, b1, e1 = carry
            hit = batch_s[0, b] == p
            one = jnp.logical_and(hit, seen == 0)
            two = jnp.logical_and(hit, seen == 1)
            local, start, end = batch_s[1, b], batch_s[2, b], batch_s[3, b]
            return (
                seen + jnp.where(hit, 1, 0),
                jnp.where(one, local, r0),
                jnp.where(one, start, b0),
                jnp.where(one, end, e0),
                jnp.where(two, local, r1),
                jnp.where(two, start, b1),
                jnp.where(two, end, e1),
            )

        zero = jnp.int32(0)
        _, r0, b0, e0, r1, b1, e1 = lax.fori_loop(0, batches, match, (zero,) * 7)
        own_s[p, 0] = r0
        own_s[p, 1] = r1
        span_s[p, 0] = b0
        span_s[p, 1] = e0
        span_s[p, 2] = b1
        span_s[p, 3] = e1
        req_out[p] = jnp.where(lane8 == 0, r0, jnp.where(lane8 == 1, r1, 0))
        return 0

    lax.fori_loop(0, npool, read_holder, 0)
    pl.semaphore_wait(
        barrier, npool - 1 + jnp.where(z > 0, 1, 0) + jnp.where(z < nz - 1, 1, 0)
    )

    def each_peer(body):
        def step(j, _):
            body(peer(j))
            return 0

        lax.fori_loop(1, npool, step, 0)

    each_peer(lambda p: req_copy(p, me).start())

    def base_block(d, s):
        part[d, s] = jnp.dot(tok[s], w[d], preferred_element_type=F32).astype(BF16)

    def end_send(d, s):
        @pl.when(first)
        def _():
            right_copy(d, s).start()

        @pl.when(last)
        def _():
            left_copy(d, s).start()

    w_copy(chunk(0)).wait()

    def first_chunk(s, _):
        tok_copy(s).wait()
        base_block(chunk(0), s)
        end_send(chunk(0), s)
        return 0

    lax.fori_loop(0, SUBS, first_chunk, 0)

    down_copy.wait()
    up_copy.wait()
    for c in range(CAP):
        down_got[me, :, c * rank2 : (c + 1) * rank2] = down[own_s[me, c]]
        up_got[pl.ds(pl.multiple_of(me * rank2 + c * rank, rank), rank), :] = up[own_s[me, c]]

    def read_request(p):
        req_copy(p, p).wait_recv()
        local = pltpu.make_async_copy(req_in.at[p], req_s.at[p], req_local.at[p])
        local.start()
        local.wait()

    each_peer(read_request)

    def serve(p):
        for c in range(CAP):
            down_send[p, :, c * rank2 : (c + 1) * rank2] = down[req_s[p, 0, c]]
            up_send[p, c * rank : (c + 1) * rank, :] = up[req_s[p, 0, c]]
        down_peer(p, me).start()
        up_peer(p, me).start()

    each_peer(serve)

    def next_chunk(i, _):
        d = chunk(i)
        w_copy(d).wait()

        def rows(s, _):
            base_block(d, s)

            @pl.when(jnp.logical_or(i < nz - 2, jnp.logical_and(i == nz - 2, s < SUBS - HELD)))
            def _():
                end_send(d, s)

            return 0

        return lax.fori_loop(0, SUBS, rows, 0)

    lax.fori_loop(1, nz, next_chunk, 0)

    shrink[...] = jnp.zeros_like(shrink)
    row_of = lax.broadcasted_iota(jnp.int32, (sub, rank2), 0)

    def down_project(p):
        def rows(s, _):
            both = jnp.dot(tok[s], down_got[p], preferred_element_type=F32)
            at = row_of + s * sub
            kept = shrink[s]
            for c in range(CAP):
                use = jnp.logical_and(at >= span_s[p, 2 * c], at < span_s[p, 2 * c + 1])
                kept = jnp.where(use, both[:, c * rank2 : (c + 1) * rank2], kept)
            shrink[s] = kept
            return 0

        lax.fori_loop(0, SUBS, rows, 0)

    def down_from(j, _):
        p = peer(j)
        down_peer(p, p).wait_recv()
        down_project(p)
        return 0

    down_project(me)
    lax.fori_loop(1, 2, down_from, 0)

    @pl.when(middle)
    def _():
        def forward(i, _):
            def rows(s, _):
                r, l = nz - 1 - i, i

                @pl.when(r > z)
                def _():
                    right_copy(r, s).wait_recv()
                    part[r, s] = (part[r, s].astype(F32) + right_in[r, s].astype(F32)).astype(BF16)
                    right_copy(r, s).start()

                @pl.when(l < z)
                def _():
                    left_copy(l, s).wait_recv()
                    part[l, s] = (part[l, s].astype(F32) + left_in[l, s].astype(F32)).astype(BF16)
                    left_copy(l, s).start()

                return 0

            return lax.fori_loop(0, SUBS, rows, 0)

        lax.fori_loop(0, nz - 1, forward, 0)

    lax.fori_loop(2, npool, down_from, 0)

    def shrink_rows(s, _):
        @pl.when(first)
        def _():
            shr_right[s] = shrink[s].astype(BF16)
            shr_right_copy(s).start()

        @pl.when(middle)
        def _():
            shr_right_copy(s).wait_recv()
            shr_right[s] = (shrink[s] + shr_right_in[s].astype(F32)).astype(BF16)
            shr_right_copy(s).start()
            shr_left_copy(s).wait_recv()
            shr_left[s] = (shrink[s] + shr_left_in[s].astype(F32)).astype(BF16)
            shr_left_copy(s).start()
            shrink[s] = (
                shrink[s] + shr_right_in[s].astype(F32) + shr_left_in[s].astype(F32)
            )

        @pl.when(last)
        def _():
            shr_left[s] = shrink[s].astype(BF16)
            shr_left_copy(s).start()

        return 0

    lax.fori_loop(0, SUBS, shrink_rows, 0)
    for s in range(SUBS - HELD, SUBS):
        end_send(chunk(nz - 2), s)

    each_peer(lambda p: up_peer(p, p).wait_recv())
    lane = lax.broadcasted_iota(jnp.int32, (sub, rank2), 1)

    def finish(s, _):
        @pl.when(first)
        def _():
            shr_left_copy(s).wait_recv()
            shrink[s] = shrink[s] + shr_left_in[s].astype(F32)

        @pl.when(last)
        def _():
            shr_right_copy(s).wait_recv()
            shrink[s] = shrink[s] + shr_right_in[s].astype(F32)

        whole = shrink[s]
        swapped = pltpu.roll(whole, rank, 1)
        half = jnp.where(lane // rank == upper, whole, swapped)
        at = row_of + s * sub
        for p in range(npool):
            begin = jnp.where(lane < rank, span_s[p, 0], span_s[p, 2])
            end = jnp.where(lane < rank, span_s[p, 1], span_s[p, 3])
            use = jnp.logical_and(at >= begin, at < end)
            mixed[:, p * rank2 : (p + 1) * rank2] = jnp.where(use, half, 0.0).astype(BF16)
        out = jnp.dot(mixed[...], up_got[...], preferred_element_type=F32)
        out_v[s] = out + part[z, s].astype(F32)

        @pl.when(z > 0)
        def _():
            right_copy(z, s).wait_recv()
            out_v[s] = out_v[s] + right_in[z, s].astype(F32)

        @pl.when(z < nz - 1)
        def _():
            left_copy(z, s).wait_recv()
            out_v[s] = out_v[s] + left_in[z, s].astype(F32)

        part[z, s] = out_v[s].astype(BF16)
        pltpu.make_async_copy(
            part.at[z, s], out_hbm.at[pl.ds(pl.multiple_of(s * sub, sub), sub)], out_sem.at[s]
        ).start()
        return 0

    lax.fori_loop(0, SUBS, finish, 0)

    def sent(s, _):
        pltpu.make_async_copy(
            part.at[z, s], out_hbm.at[pl.ds(pl.multiple_of(s * sub, sub), sub)], out_sem.at[s]
        ).wait()

        def one(d, _):
            @pl.when(d > z)
            def _():
                right_copy(d, s).wait_send()

            @pl.when(d < z)
            def _():
                left_copy(d, s).wait_send()

            return 0

        lax.fori_loop(0, nz, one, 0)

        @pl.when(z < nz - 1)
        def _():
            shr_right_copy(s).wait_send()

        @pl.when(z > 0)
        def _():
            shr_left_copy(s).wait_send()

        return 0

    lax.fori_loop(0, SUBS, sent, 0)

    def pool_sent(p):
        req_copy(p, me).wait_send()
        down_peer(p, me).wait_send()
        up_peer(p, me).wait_send()

    each_peer(pool_sent)


def body(tokens, base_w, down_w, up_w, ids, counts, row_table):
    nz, npool = lax.axis_size("tensor"), lax.axis_size("pool")
    rows, features = tokens.shape
    slots, _, rank2 = down_w.shape
    rank, cw = up_w.shape[1:]
    batches = ids.shape[1]
    sub = rows // SUBS
    any_spec = pl.BlockSpec(memory_space=pl.ANY)
    smem = pl.BlockSpec(memory_space=pltpu.SMEM)
    dma = pltpu.SemaphoreType.DMA
    vmem = pltpu.VMEM
    return pl.pallas_call(
        functools.partial(kernel, nz, npool),
        out_shape=jax.ShapeDtypeStruct((rows, cw), BF16),
        in_specs=[any_spec] * 4 + [smem] * 3,
        out_specs=any_spec,
        scratch_shapes=[
            vmem((SUBS, sub, features), BF16),
            vmem((nz, features, cw), BF16),
            vmem((slots, features, rank2), BF16),
            vmem((slots, rank, cw), BF16),
            vmem((nz, SUBS, sub, cw), BF16),
            vmem((nz, SUBS, sub, cw), BF16),
            vmem((nz, SUBS, sub, cw), BF16),
            vmem((npool, features, CAP * rank2), BF16),
            vmem((npool, features, CAP * rank2), BF16),
            vmem((npool, CAP * rank, cw), BF16),
            vmem((npool * CAP * rank, cw), BF16),
            vmem((SUBS, sub, rank2), F32),
            vmem((SUBS, sub, rank2), BF16),
            vmem((SUBS, sub, rank2), BF16),
            vmem((SUBS, sub, rank2), BF16),
            vmem((SUBS, sub, rank2), BF16),
            vmem((sub, npool * CAP * rank), BF16),
            vmem((SUBS, sub, cw), F32),
            vmem((npool, 8, 128), jnp.int32),
            vmem((npool, 8, 128), jnp.int32),
            pltpu.SMEM((npool, 8, 128), jnp.int32),
            pltpu.SMEM((npool, CAP), jnp.int32),
            pltpu.SMEM((npool, 2 * CAP), jnp.int32),
            pltpu.SMEM((4, batches), jnp.int32),
            dma((SUBS,)),
            dma((nz,)),
            dma,
            dma,
            dma((SUBS,)),
            dma((nz, SUBS)),
            dma((nz, SUBS)),
            dma((nz, SUBS)),
            dma((npool,)),
            dma((npool,)),
            dma((npool,)),
            dma((npool,)),
            dma((npool,)),
            dma((npool,)),
            dma((npool,)),
            dma((2, SUBS)),
            dma((SUBS,)),
            dma((SUBS,)),
        ],
        compiler_params=pltpu.CompilerParams(
            collective_id=0, has_side_effects=True, vmem_limit_bytes=54 * 1024 * 1024
        ),
    )(tokens, base_w, down_w, up_w, ids, counts, row_table)


def solution(mesh):
    in_specs = (
        P(("group", "pool"), "tensor"),
        P("tensor", None),
        P(("group", "pool"), "tensor", None),
        P(("group", "pool"), None, "tensor"),
        P(("group", "pool"), None),
        P(("group", "pool"), None),
        P("group"),
    )
    out_specs = P(("group", "pool"), "tensor")
    return jax.shard_map(body, mesh=mesh, in_specs=in_specs, out_specs=out_specs, check_vma=False)
```

time: 286 us -> 124 us (0.43)
  Pallas kernels: 0 us -> 121 us
  local copies, waits for them, and re-layouts: 78.2 us -> 2.26 us
  loops' own time: 62.1 us -> 0 us
  waiting for transfers between devices: 59.8 us -> 0 us
  matrix products: 39.1 us -> 0 us
  other arithmetic: 14.7 us -> 0 us
  between operations: 13.5 us -> 0.01 us
  starting transfers between devices: 8.56 us -> 0 us
  blocking collectives: 7.76 us -> 0 us
    pallas_call x0 -> x1, Pallas kernels: none -> 121 us  [body(): pl.pallas_call(functools.partial(kernel, nz, npool), out_shape=jax.ShapeD...]
    another operation x2 -> x0, loops' own time: 62.1 us -> none  [the longest x1 31.3 us: body(): lax.fori_loop(0, batches, expand_step, jnp.zeros((tok_rows + max_rows, ou...]
    all_to_all x2 -> x0, waiting for transfers between devices: 42.8 us -> none  [the longest x1 42.8 us: body(): lax.all_to_all(adapter_down_weight[requested_adapter], 'pool', split_axis...]
    dot_general x17 -> x0, matrix products: 39.1 us -> none  [the longest x8 14.5 us: segment_shrink(): return jnp.dot(segment, adapter_block, preferred_element_type=jnp.float32)]
    dynamic_update_slice x16 -> x0, local copies, waits for them, and re-layouts: 31.2 us -> none  [place_rows(): lax.dynamic_update_slice_in_dim(running_totals, prior_count + jnp.where(w...]
    dynamic_slice x48 -> x0, local copies, waits for them, and re-layouts: 29.8 us -> none  [the longest x8 5.25 us: segment_shrink(): flat_slot[batch_position]]
    psum x1 -> x0, waiting for transfers between devices: 17 us -> none  [body(): shared = lax.psum(shrink_totals[:tok_rows].astype(jnp.bfloat16), 'tensor')]
    lt x16 -> x0, other arithmetic: 10.3 us -> none  [place_rows(): within_batch = (jnp.arange(values.shape[0]) < length)[:, None]]
  transfers between devices with their start and end apart: 4 -> 0, of which waited for: 2 -> 0; matrix products, arithmetic and copies ran while one was open for 27% -> 0% of each run, Pallas kernels for 0% -> 0%
where the time goes in v1:
time: 124 us; the launch traced here: 123 us
  Pallas kernels  121 us (98%)
  local copies, waits for them, and re-layouts  2.26 us (2%)
    pallas_call x1, Pallas kernels, body(): pl.pallas_call(functools.partial(kernel, nz, npool), out_shape=jax.ShapeD...  121 us

profile of v1, /device:TPU:0, one launch (start us, length us, event | category | flops | bytes accessed | tf_op | source)
XLA Modules:
  0.0 123.4 jit_solution(10078505493007304861)
XLA Ops:
  0.0 121.1 %shard_map.73 = bf16[1024,512]{1,0:T(8,128)(2,1)} custom-call(bf16[1024,2048]{1,0:T(8,128)(2,1)} %tok_hbm.1, bf16[2048,2048]{1,0:T(8,128)(2,1)} %w_hbm.1, bf16[8,2048,128]{2,1,0:T(8,128)(2,1)} %down_hbm.1, bf16[8,64,512]{2,1,0:T(8,128)(2,1)} %up_hbm.1, s32[1,8]{1,0:T(1,128)} %ids.1, s32[1,8]{1,0:T(1,128)} %counts.1, s32[32]{0:T(128)} %row_table.1), custom_call_target="tpu_custom_call" | custom-call | tf_op jit(solution)/shard_map/pallas_call | solution.py:479
  121.1 2.3 %copy.9 = bf16[1024,512]{1,0:T(8,128)(2,1)} copy(bf16[1024,512]{1,0:T(8,128)(2,1)} %shard_map.73) | data formatting | bytes 2097152

commit v2 on v1

--- a/solution.py
+++ b/solution.py
@@ -39,10 +39,8 @@
     up_send,
     up_got,
     shrink,
-    shr_right,
-    shr_left,
-    shr_right_in,
-    shr_left_in,
+    shr_pack,
+    shr_in,
     mixed,
     out_v,
     req_out,
@@ -67,8 +65,7 @@
     up_send_sem,
     up_recv,
     shr_send_sem,
-    shr_right_recv,
-    shr_left_recv,
+    shr_recv,
 ):
     z = lax.axis_index("tensor")
     me = lax.axis_index("pool")
@@ -119,23 +116,13 @@
             device_id_type=MESH,
         )
 
-    def shr_right_copy(s):
+    def shr_copy(to, landing):
         return pltpu.make_async_remote_copy(
-            src_ref=shr_right.at[s],
-            dst_ref=shr_right_in.at[s],
-            send_sem=shr_send_sem.at[0, s],
-            recv_sem=shr_right_recv.at[s],
-            device_id={"tensor": z + 1},
-            device_id_type=MESH,
-        )
-
-    def shr_left_copy(s):
-        return pltpu.make_async_remote_copy(
-            src_ref=shr_left.at[s],
-            dst_ref=shr_left_in.at[s],
-            send_sem=shr_send_sem.at[1, s],
-            recv_sem=shr_left_recv.at[s],
-            device_id={"tensor": z - 1},
+            src_ref=shr_pack.at[lax.div(2 * to, nz)],
+            dst_ref=shr_in.at[landing],
+            send_sem=shr_send_sem.at[to],
+            recv_sem=shr_recv.at[landing],
+            device_id={"tensor": to},
             device_id_type=MESH,
         )
 
@@ -175,13 +162,13 @@
 
     barrier = pltpu.get_barrier_semaphore()
 
-    @pl.when(z > 0)
-    def _():
-        pl.semaphore_signal(barrier, inc=1, device_id={"tensor": z - 1}, device_id_type=MESH)
-
-    @pl.when(z < nz - 1)
-    def _():
-        pl.semaphore_signal(barrier, inc=1, device_id={"tensor": z + 1}, device_id_type=MESH)
+    def line_peer(j):
+        return lax.rem(z + j, nz)
+
+    for j in range(1, nz):
+        pl.semaphore_signal(
+            barrier, inc=1, device_id={"tensor": line_peer(j)}, device_id_type=MESH
+        )
 
     for j in range(1, npool):
         p = peer(jnp.int32(j))
@@ -228,9 +215,7 @@
         return 0
 
     lax.fori_loop(0, npool, read_holder, 0)
-    pl.semaphore_wait(
-        barrier, npool - 1 + jnp.where(z > 0, 1, 0) + jnp.where(z < nz - 1, 1, 0)
-    )
+    pl.semaphore_wait(barrier, npool - 1 + nz - 1)
 
     def each_peer(body):
         def step(j, _):
@@ -330,76 +315,64 @@
 
     @pl.when(middle)
     def _():
-        def forward(i, _):
-            def rows(s, _):
-                r, l = nz - 1 - i, i
-
-                @pl.when(r > z)
-                def _():
-                    right_copy(r, s).wait_recv()
-                    part[r, s] = (part[r, s].astype(F32) + right_in[r, s].astype(F32)).astype(BF16)
-                    right_copy(r, s).start()
-
-                @pl.when(l < z)
-                def _():
-                    left_copy(l, s).wait_recv()
-                    part[l, s] = (part[l, s].astype(F32) + left_in[l, s].astype(F32)).astype(BF16)
-                    left_copy(l, s).start()
-
-                return 0
-
-            return lax.fori_loop(0, SUBS, rows, 0)
-
-        lax.fori_loop(0, nz - 1, forward, 0)
+        def forward(t, _):
+            right_at, left_at = t - z, t - (nz - 1 - z)
+            r, rs = nz - 1 - lax.div(right_at, SUBS), lax.rem(right_at, SUBS)
+            l, ls = lax.div(left_at, SUBS), lax.rem(left_at, SUBS)
+
+            @pl.when(jnp.logical_and(right_at >= 0, r > z))
+            def _():
+                right_copy(r, rs).wait_recv()
+                part[r, rs] = (part[r, rs].astype(F32) + right_in[r, rs].astype(F32)).astype(BF16)
+                right_copy(r, rs).start()
+
+            @pl.when(jnp.logical_and(left_at >= 0, l < z))
+            def _():
+                left_copy(l, ls).wait_recv()
+                part[l, ls] = (part[l, ls].astype(F32) + left_in[l, ls].astype(F32)).astype(BF16)
+                left_copy(l, ls).start()
+
+            return 0
+
+        lax.fori_loop(0, (nz - 2) * SUBS + 1, forward, 0)
 
     lax.fori_loop(2, npool, down_from, 0)
 
-    def shrink_rows(s, _):
-        @pl.when(first)
-        def _():
-            shr_right[s] = shrink[s].astype(BF16)
-            shr_right_copy(s).start()
-
-        @pl.when(middle)
-        def _():
-            shr_right_copy(s).wait_recv()
-            shr_right[s] = (shrink[s] + shr_right_in[s].astype(F32)).astype(BF16)
-            shr_right_copy(s).start()
-            shr_left_copy(s).wait_recv()
-            shr_left[s] = (shrink[s] + shr_left_in[s].astype(F32)).astype(BF16)
-            shr_left_copy(s).start()
-            shrink[s] = (
-                shrink[s] + shr_right_in[s].astype(F32) + shr_left_in[s].astype(F32)
-            )
-
-        @pl.when(last)
-        def _():
-            shr_left[s] = shrink[s].astype(BF16)
-            shr_left_copy(s).start()
-
+    lane = lax.broadcasted_iota(jnp.int32, (sub, rank2), 1)
+
+    def pack(s, _):
+        a, b = shrink[s], shrink[s + SUBS // 2]
+        shr_pack[0, s] = jnp.where(lane < rank, a, pltpu.roll(b, rank, 1)).astype(BF16)
+        shr_pack[1, s] = jnp.where(lane < rank, pltpu.roll(a, rank, 1), b).astype(BF16)
         return 0
 
-    lax.fori_loop(0, SUBS, shrink_rows, 0)
+    lax.fori_loop(0, SUBS // 2, pack, 0)
+
+    def each_line_peer(body):
+        def step(j, _):
+            body(line_peer(j))
+            return 0
+
+        lax.fori_loop(1, nz, step, 0)
+
+    each_line_peer(lambda to: shr_copy(to, z).start())
     for s in range(SUBS - HELD, SUBS):
         end_send(chunk(nz - 2), s)
 
     each_peer(lambda p: up_peer(p, p).wait_recv())
-    lane = lax.broadcasted_iota(jnp.int32, (sub, rank2), 1)
+    each_line_peer(lambda p: shr_copy(p, p).wait_recv())
+    for s in range(SUBS // 2):
+        shrink[s] = shr_pack[upper, s].astype(F32)
+
+        def add(p, s=s):
+            shrink[s] = shrink[s] + shr_in[p, s].astype(F32)
+
+        each_line_peer(add)
 
     def finish(s, _):
-        @pl.when(first)
-        def _():
-            shr_left_copy(s).wait_recv()
-            shrink[s] = shrink[s] + shr_left_in[s].astype(F32)
-
-        @pl.when(last)
-        def _():
-            shr_right_copy(s).wait_recv()
-            shrink[s] = shrink[s] + shr_right_in[s].astype(F32)
-
-        whole = shrink[s]
-        swapped = pltpu.roll(whole, rank, 1)
-        half = jnp.where(lane // rank == upper, whole, swapped)
+        packed = shrink[lax.rem(s, SUBS // 2)]
+        swapped = pltpu.roll(packed, rank, 1)
+        half = jnp.where(lane // rank == lax.div(s, SUBS // 2), packed, swapped)
         at = row_of + s * sub
         for p in range(npool):
             begin = jnp.where(lane < rank, span_s[p, 0], span_s[p, 2])
@@ -445,14 +418,6 @@
 
         lax.fori_loop(0, nz, one, 0)
 
-        @pl.when(z < nz - 1)
-        def _():
-            shr_right_copy(s).wait_send()
-
-        @pl.when(z > 0)
-        def _():
-            shr_left_copy(s).wait_send()
-
         return 0
 
     lax.fori_loop(0, SUBS, sent, 0)
@@ -463,6 +428,7 @@
         up_peer(p, me).wait_send()
 
     each_peer(pool_sent)
+    each_line_peer(lambda to: shr_copy(to, z).wait_send())
 
 
 def body(tokens, base_w, down_w, up_w, ids, counts, row_table):
@@ -494,10 +460,8 @@
             vmem((npool, CAP * rank, cw), BF16),
             vmem((npool * CAP * rank, cw), BF16),
             vmem((SUBS, sub, rank2), F32),
-            vmem((SUBS, sub, rank2), BF16),
-            vmem((SUBS, sub, rank2), BF16),
-            vmem((SUBS, sub, rank2), BF16),
-            vmem((SUBS, sub, rank2), BF16),
+            vmem((2, SUBS // 2, sub, rank2), BF16),
+            vmem((nz, SUBS // 2, sub, rank2), BF16),
             vmem((sub, npool * CAP * rank), BF16),
             vmem((SUBS, sub, cw), F32),
             vmem((npool, 8, 128), jnp.int32),
@@ -521,9 +485,8 @@
             dma((npool,)),
             dma((npool,)),
             dma((npool,)),
-            dma((2, SUBS)),
-            dma((SUBS,)),
-            dma((SUBS,)),
+            dma((nz,)),
+            dma((nz,)),
         ],
         compiler_params=pltpu.CompilerParams(
             collective_id=0, has_side_effects=True, vmem_limit_bytes=54 * 1024 * 1024

time: 124 us -> 87.1 us (0.70)
  Pallas kernels: 121 us -> 84.7 us
    pallas_call x1, Pallas kernels: 121 us -> 84.7 us  [body(): pl.pallas_call(functools.partial(kernel, nz, npool), out_shape=jax.ShapeD...]
where the time goes in v2:
time: 87.1 us; the launch traced here: 87 us
  Pallas kernels  84.7 us (97%)
  local copies, waits for them, and re-layouts  2.26 us (3%)
    pallas_call x1, Pallas kernels, body(): pl.pallas_call(functools.partial(kernel, nz, npool), out_shape=jax.ShapeD...  84.7 us
    unnamed x1, local copies, waits for them, and re-layouts  2.26 us

profile of v2, /device:TPU:0, one launch (start us, length us, event | category | flops | bytes accessed | tf_op | source)
XLA Modules:
  0.0 87.0 jit_solution(1924826403427244132)
XLA Ops:
  0.0 84.7 %shard_map.73 = bf16[1024,512]{1,0:T(8,128)(2,1)} custom-call(bf16[1024,2048]{1,0:T(8,128)(2,1)} %tok_hbm.1, bf16[2048,2048]{1,0:T(8,128)(2,1)} %w_hbm.1, bf16[8,2048,128]{2,1,0:T(8,128)(2,1)} %down_hbm.1, bf16[8,64,512]{2,1,0:T(8,128)(2,1)} %up_hbm.1, s32[1,8]{1,0:T(1,128)} %ids.1, s32[1,8]{1,0:T(1,128)} %counts.1, s32[32]{0:T(128)} %row_table.1), custom_call_target="tpu_custom_call" | custom-call | tf_op jit(solution)/shard_map/pallas_call | solution.py:445
  84.7 2.3 %copy.9 = bf16[1024,512]{1,0:T(8,128)(2,1)} copy(bf16[1024,512]{1,0:T(8,128)(2,1)} %shard_map.73) | data formatting | bytes 2097152

commit v3 on v2

--- a/solution.py
+++ b/solution.py
@@ -9,8 +9,8 @@
 
 DRAFT = 8
 CAP = 2
-SUBS = 4
-HELD = 2
+SUBS = 2
+HELD = 1
 MESH = pl.DeviceIdType.MESH
 F32 = jnp.float32
 BF16 = jnp.bfloat16
@@ -350,7 +350,7 @@
 
     def each_line_peer(body):
         def step(j, _):
-            body(line_peer(j))
+            body(line_peer(j + (1 - upper) * (nz - 2 * j)))
             return 0
 
         lax.fori_loop(1, nz, step, 0)

time: 87.1 us -> 86.6 us (level); the launches traced: 87 us -> 85.3 us
  Pallas kernels: 84.7 us -> 83 us
    pallas_call x1, Pallas kernels: 84.7 us -> 83 us  [body(): pl.pallas_call(functools.partial(kernel, nz, npool), out_shape=jax.ShapeD...]
where the time goes in v3:
time: 86.6 us; the launch traced here: 85.3 us
  Pallas kernels  83 us (96%)
  local copies, waits for them, and re-layouts  2.26 us (3%)
    pallas_call x1, Pallas kernels, body(): pl.pallas_call(functools.partial(kernel, nz, npool), out_shape=jax.ShapeD...  83 us
    unnamed x1, local copies, waits for them, and re-layouts  2.26 us

profile of v3, /device:TPU:0, one launch (start us, length us, event | category | flops | bytes accessed | tf_op | source)
XLA Modules:
  0.0 85.3 jit_solution(9202790449884986828)
XLA Ops:
  0.0 83.0 %shard_map.73 = bf16[1024,512]{1,0:T(8,128)(2,1)} custom-call(bf16[1024,2048]{1,0:T(8,128)(2,1)} %tok_hbm.1, bf16[2048,2048]{1,0:T(8,128)(2,1)} %w_hbm.1, bf16[8,2048,128]{2,1,0:T(8,128)(2,1)} %down_hbm.1, bf16[8,64,512]{2,1,0:T(8,128)(2,1)} %up_hbm.1, s32[1,8]{1,0:T(1,128)} %ids.1, s32[1,8]{1,0:T(1,128)} %counts.1, s32[32]{0:T(128)} %row_table.1), custom_call_target="tpu_custom_call" | custom-call | tf_op jit(solution)/shard_map/pallas_call | solution.py:445
  83.0 2.3 %copy.9 = bf16[1024,512]{1,0:T(8,128)(2,1)} copy(bf16[1024,512]{1,0:T(8,128)(2,1)} %shard_map.73) | data formatting | bytes 2097152
